TPU v7x, 32 devices: a whole 2x2x4 slice. The times are simulated.
32 devices in a mesh: col: 8 (over y, x, core), row: 4 (over z).
Axes of the slice: x: 2, y: 2, z: 4, core: 2. Of those that a mesh axis runs over, the one named last changes fastest.
Arguments:
- normal_matrix: float32 [4, 4, 128, 2, 8, 128], P(None, 'row', None, None, 'col'), may hold values from -3 to 5.5, as said below
- right_sides: float32 [64, 4, 4, 128], P('col', None, 'row'), may hold values from -6 to 6
Outputs:
- reduced_matrix: float32 [4, 4, 128, 2, 8, 128], P(None, 'row', None, None, 'col')
- reduced_sides: float32 [64, 4, 4, 128], P('col', None, 'row')
Inputs may be any that keep to these rules, and one draw needn't show every extreme that they name: `normal_matrix`: A is symmetric; its leading 128 x 128 block is strictly diagonally dominant with a positive diagonal.
All inputs are finite; a program needn't handle non-finite values.
Results may differ from a plain program's by a relative error of at most 0.00005.
Values sent between devices are 32-bit elements; how exact they have to be, the bound alone decides.
A program may use at most 64 MiB of HBM per device.

v0:
```python
import jax
import jax.numpy as jnp
from jax import lax
from jax.sharding import PartitionSpec as P


def spread(block, axis, holder):
    block = jnp.where(lax.axis_index(axis) == holder, block, jnp.zeros_like(block))
    return lax.psum(block, axis)


def on_device(normal_matrix, right_sides):
    row_blocks, _, block, col_blocks, _, _ = normal_matrix.shape
    col_id = lax.axis_index("col")
    row_id = lax.axis_index("row")
    col_count = lax.axis_size("col")
    row_count = lax.axis_size("row")
    local = normal_matrix.reshape(row_blocks * block, col_blocks * block)
    first = local[:, :block]
    corner_raw = spread(first[:block], "row", 0)
    identity = jnp.eye(block, dtype=jnp.float32)
    corner_raw = jnp.where(col_id == 0, corner_raw, identity)
    corner_own = jnp.linalg.cholesky(corner_raw)
    rows_own = jax.scipy.linalg.solve_triangular(corner_own, first.T, lower=True).T
    stacked = jnp.concatenate([corner_own, rows_own], axis=0)
    stacked = spread(stacked, "col", 0)
    corner = stacked[:block]
    rows_factor = stacked[block:]
    picked = []
    for index in range(col_blocks):
        start = (index * col_count + col_id) // row_count * block
        picked.append(lax.dynamic_slice_in_dim(rows_factor, start, block, 0))
    selected = jnp.concatenate(picked, axis=0)
    cols_factor = spread(selected, "row", col_id % row_count)
    change = jnp.dot(
        rows_factor,
        cols_factor.T,
        precision=lax.Precision.HIGHEST,
        preferred_element_type=jnp.float32,
    )
    trailing = (local - change).reshape(row_blocks, block, col_blocks, block)
    global_rows = row_id + row_count * jnp.arange(row_blocks, dtype=jnp.int32)
    global_cols = col_id + col_count * jnp.arange(col_blocks, dtype=jnp.int32)
    inner = (global_rows[:, None, None, None] >= 1) & (global_cols[None, None, :, None] >= 1)
    result = jnp.where(inner, trailing, jnp.float32(0.0))
    column = jnp.where(
        global_rows[:, None, None] == 0, corner[None], rows_factor.reshape(row_blocks, block, block)
    )
    result = jnp.where((global_cols == 0)[None, None, :, None], column[:, :, None, :], result)
    result = result.reshape(normal_matrix.shape)
    side_count = right_sides.shape[0]
    top_sides = spread(right_sides[:, 0, 0, :], "row", 0)
    lead = jax.scipy.linalg.solve_triangular(corner, top_sides.T, lower=True).T
    flat = right_sides.reshape(side_count, row_blocks * block)
    reduced = flat - jnp.dot(
        lead, rows_factor.T, precision=lax.Precision.HIGHEST, preferred_element_type=jnp.float32
    )
    reduced = reduced.reshape(side_count, row_blocks, block)
    reduced = jnp.where((global_rows == 0)[None, :, None], lead[:, None, :], reduced)
    return (result, reduced.reshape(right_sides.shape))


def solution(mesh):
    placed = (P(None, "row", None, None, "col", None), P("col", None, "row", None))
    return jax.shard_map(
        on_device,
        mesh=mesh,
        in_specs=placed,
        out_specs=(P(None, "row", None, None, "col", None), P("col", None, "row", None)),
        check_vma=False,
    )
```

profile of v0, /device:TPU:0, one launch (start us, length us, event | category | flops | bytes accessed | tf_op | source)
XLA Modules:
  0.0 182.4 jit_solution(6530600031602383277)
XLA Ops:
  7.2 0.0 all-reduce.4.cloned.1.call-start
  7.2 1.1 copy.16
  8.3 0.6 slice_select_fusion
  9.0 0.0 all-reduce.6.cloned.1.call-start
  9.0 0.6 copy-done.3
  9.7 0.1 broadcast_and_fusion
  9.7 37.8 %all-reduce.4.cloned.1.call-done = f32[128,128]{1,0:T(8,128)} async-done(((f32[128,128]{1,0:T(8,128)}), f32[128,128]{1,0:T(8,128)}) %all-reduce.4.cloned.1.call-update) | async-done | bytes 65552 | tf_op jit(solution)/shard_map/psum | solution.py:9
  47.6 0.9 convert_select_fusion
  48.5 0.1 copy.4
  48.6 0.7 copy-done.2
  49.3 11.7 %cholesky.19 = f32[128,128]{1,0:T(8,128)S(1)} custom-call(f32[128,128]{1,0:T(8,128)S(1)} %fusion.5), custom_call_target="Cholesky" | custom-call | tf_op jit(solution)/shard_map/jit(cholesky)/cholesky | solution.py:23
  61.1 0.6 compare_reduce_fusion
  61.7 0.7 select_bitcast_fusion.1
  62.4 9.8 %custom-call.11 = f32[1,128,128]{1,2,0:T(8,128)S(1)} custom-call(f32[1,128,128]{2,1,0:T(8,128)S(1)} %get-tuple-element.2), custom_call_target="InvertDiagBlocksLowerTriangular" | custom-call | tf_op jit(solution)/shard_map/jit(_solve_triangular)/triangular_solve | solution.py:24
  72.2 0.4 convolution_bitcast_fusion
  72.6 0.7 maximum_select_fusion
  73.3 0.0 all-reduce.8.cloned.1.call-start
  73.4 10.5 %psum.31 = f32[8,128]{1,0:T(8,128)S(1)} all-reduce(f32[8,128]{1,0:T(8,128)S(1)} %bitcast.46), channel_id=1, replica_groups=mesh['col'=8,'row'=4] {'row'}, use_global_device_ids=true, to_apply=%region_5.6 | all-reduce | flops 1024 | bytes 8192 | tf_op jit(solution)/shard_map/psum | solution.py:9
  83.9 42.3 %all-reduce.6.cloned.1.call-done = f32[640,128]{1,0:T(8,128)} async-done(((f32[640,128]{1,0:T(8,128)}), f32[640,128]{1,0:T(8,128)}) %all-reduce.6.cloned.1.call-update) | async-done | bytes 327696 | tf_op jit(solution)/shard_map/psum | solution.py:9
  126.2 0.8 select_bitcast_fusion
  127.1 9.8 %custom-call.12 = f32[1,128,128]{1,2,0:T(8,128)S(1)} custom-call(f32[1,128,128]{2,1,0:T(8,128)S(1)} %get-tuple-element.4), custom_call_target="InvertDiagBlocksLowerTriangular" | custom-call | tf_op jit(solution)/shard_map/jit(_solve_triangular)/triangular_solve | solution.py:53
  136.9 1.0 slice.42
  137.9 0.7 maximum_select_fusion.1
  138.6 0.2 fusion.2
  138.8 0.1 broadcast_select_fusion.2
  138.9 0.7 copy-done
  139.6 0.3 fusion
  139.9 0.7 broadcast_select_fusion.3
  140.6 32.0 %all-reduce.8.cloned.1.call-done = f32[256,128]{1,0:T(8,128)} async-done(((f32[256,128]{1,0:T(8,128)}), f32[256,128]{1,0:T(8,128)}) %all-reduce.8.cloned.1.call-update) | async-done | bytes 131088 | tf_op jit(solution)/shard_map/psum | solution.py:9
  172.6 1.5 convolution_subtract_fusion
  174.1 0.3 reshape.136
  174.3 1.5 broadcast_select_fusion
  (16 shorter events, 0.2 us)
Async XLA Ops:
  7.2 40.4 %all-reduce.4.cloned.1.call-start = ((), (), s32[]{:S(2)}) async-start(), calls=%async_computation | async-start | bytes 131072 | tf_op jit(solution)/shard_map/psum | solution.py:9
  8.9 0.7 copy-start.3
  9.0 117.3 %all-reduce.6.cloned.1.call-start = ((), (), s32[]{:S(2)}) async-start(), calls=%async_computation.1 | async-start | bytes 655360 | tf_op jit(solution)/shard_map/psum | solution.py:9
  48.5 0.8 copy-start.2
  73.3 99.2 %all-reduce.8.cloned.1.call-start = ((), (), s32[]{:S(2)}) async-start(), calls=%async_computation.2 | async-start | bytes 262144 | tf_op jit(solution)/shard_map/psum | solution.py:9
  138.6 1.0 copy-start
  138.6 34.0 %copy-start.1 = (f32[4,1,128,2,1,128]{5,4,3,2,1,0:T(1,128)S(1)}, f32[4,1,128,2,1,128]{5,4,3,2,1,0:T(1,128)}, u32[]{:S(2)}) copy-start(f32[4,1,128,2,1,128]{5,4,3,2,1,0:T(1,128)} %param.2) | copy-start | bytes 1572868
Sparse Core Ops, SparseCore 0:
  10.9 36.6 all-reduce.3
  73.5 52.7 all-reduce.5
  138.7 33.8 all-reduce.7
where the time goes:
time: 183 us; the launch traced here: 182 us
  waiting for transfers between devices  112 us (61%)
  other arithmetic  38.9 us (21%)
  between operations  13.9 us (8%)
  blocking collectives  10.5 us (6%)
  local copies, waits for them, and re-layouts  4.48 us (2%)
  matrix products  2.31 us (1%)
    psum x3, waiting for transfers between devices, spread(): return lax.psum(block, axis)  112 us
    another operation x3, other arithmetic, on_device(): corner_own = jnp.linalg.cholesky(corner_raw)  12.4 us
    another operation x2, other arithmetic, on_device(): lead = jax.scipy.linalg.solve_triangular(corner, top_sides.T, lower=True).T  10.7 us
    psum x1, blocking collectives, spread(): return lax.psum(block, axis)  10.5 us
    another operation x2, other arithmetic, on_device(): jax.scipy.linalg.solve_triangular(corner_own, first.T, lower=True)  10.5 us
  transfers between devices with their start and end apart: 3, of which 3 were waited for; matrix products, arithmetic and copies ran while one was open for 1% of the time, Pallas kernels for 0%

commit v1 on v0

v1 whole, which is shorter than its diff:
```python
import functools

import jax
import jax.numpy as jnp
from jax import lax
from jax.experimental import pallas as pl
from jax.experimental.pallas import tpu as pltpu
from jax.sharding import PartitionSpec as P

F32 = jnp.float32


def dot(a, b, dims):
    return lax.dot_general(
        a, b, (dims, ((), ())), precision=lax.Precision.HIGHEST, preferred_element_type=F32
    )


def eliminate(first, second):
    count = len(first)
    shape = first[0].shape
    sub = lax.broadcasted_iota(jnp.int32, shape, 0)
    first, second = list(first), list(second)
    for b in range(count):
        cols = [
            [jnp.broadcast_to(first[t][:, 8 * b + i : 8 * b + i + 1], shape) for i in range(8)]
            for t in range(b, count)
        ]
        e = [[None] * 8 for _ in range(8)]
        for i in range(8):
            for j in range(i + 1):
                e[j][i] = jnp.broadcast_to(cols[0][i][j : j + 1, :], shape)
        rows1 = [jnp.broadcast_to(first[b][j : j + 1, :], shape) for j in range(8)]
        rows2 = [jnp.broadcast_to(second[b][j : j + 1, :], shape) for j in range(8)]
        for k in range(8):
            scale = lax.rsqrt(e[k][k])
            low = {j: e[k][j] * scale for j in range(k + 1, 8)}
            for i in range(k + 1, 8):
                for j in range(k + 1, i + 1):
                    e[j][i] = e[j][i] - low[j] * low[i]
            rows1[k] = rows1[k] * scale
            rows2[k] = rows2[k] * scale
            for j in range(k + 1, 8):
                rows1[j] = rows1[j] - low[j] * rows1[k]
                rows2[j] = rows2[j] - low[j] * rows2[k]
            for t in range(b + 1, count):
                c = cols[t - b]
                c[k] = c[k] * scale
                for j in range(k + 1, 8):
                    c[j] = c[j] - low[j] * c[k]
                first[t] = first[t] - c[k] * rows1[k]
                second[t] = second[t] - c[k] * rows2[k]
        done1, done2 = rows1[0], rows2[0]
        for k in range(1, 8):
            done1 = jnp.where(sub == k, rows1[k], done1)
            done2 = jnp.where(sub == k, rows2[k], done2)
        first[b], second[b] = done1, done2
    return jnp.concatenate(first, axis=0), jnp.concatenate(second, axis=0)


def groups(x):
    return [x[8 * t : 8 * t + 8] for t in range(x.shape[0] // 8)]


def kernel(
    sizes, a_ref, b_ref, out_ref, red_ref,
    ybuf, zbuf, tbuf, wbuf, ubuf,
    ysend, yrecv, zsend, zrecv, wrow, wcol, wrecv,
):
    row_count, col_count, rb, cb, nb, sides = sizes
    half = nb // 2
    r = lax.axis_index("row")
    c = lax.axis_index("col")
    bits = max(1, (col_count - 1).bit_length())
    root = (r == 0) & (c == 0)
    sends_down = [
        (lax.rem(c, 2 ** (b + 1)) == 0) & (c + 2**b < col_count) for b in range(bits)
    ]
    parent = c * 0
    for b in range(bits):
        parent = jnp.where(lax.rem(c, 2 ** (b + 1)) == 2**b, c - 2**b, parent)

    @pl.when(c == 0)
    def _():
        for i in range(rb):
            ybuf[i] = a_ref[pl.ds(i * nb * cb, nb, stride=cb), :]

    @pl.when(r == 0)
    def _():
        for j in range(cb):
            zbuf[j] = a_ref[pl.ds(j, nb, stride=cb), :]
        tbuf[...] = b_ref[pl.ds(0, sides, stride=rb), :]

    barrier = pltpu.get_barrier_semaphore()

    def greet(row, col):
        pl.semaphore_signal(
            barrier, inc=1, device_id={"row": row, "col": col}, device_id_type=pl.DeviceIdType.MESH
        )

    @pl.when(c != 0)
    def _():
        greet(r, parent)
        greet(r, 0)

    @pl.when(r != 0)
    def _():
        greet(r - 1, c)

    @pl.when((r != 0) & (c == 0))
    def _():
        greet(0, 0)

    targets = jnp.where(r < row_count - 1, 1, 0)
    for b in range(bits):
        targets = targets + jnp.where(sends_down[b], 1, 0)
    targets = targets + jnp.where(c == 0, col_count - 1, 0)
    targets = targets + jnp.where(root, row_count - 1, 0)

    @pl.when(targets > 0)
    def _():
        pl.semaphore_wait(barrier, targets)

    def copy(ref, send, recv, row, col):
        return pltpu.make_async_remote_copy(
            src_ref=ref,
            dst_ref=ref,
            send_sem=send,
            recv_sem=recv,
            device_id={"row": row, "col": col},
            device_id_type=pl.DeviceIdType.MESH,
        )

    def y_copy(i, b):
        return copy(ybuf.at[i], ysend.at[b, i], yrecv.at[i], r, c + 2**b)

    def z_copy(j):
        ref = zbuf.at[j] if j < cb else tbuf
        return copy(ref, zsend.at[j], zrecv.at[j], r + 1, c)

    def w_row(p, row):
        return copy(wbuf.at[p], wrow.at[row, p], wrecv.at[p], row, 0)

    def w_col(p, col):
        return copy(wbuf.at[p], wcol.at[col, p], wrecv.at[p], r, col)

    for i in range(max(rb, cb + 1)):
        if i < rb:
            @pl.when(c != 0)
            def _(i=i):
                y_copy(i, 0).wait_recv()

            for b in reversed(range(bits)):
                @pl.when(sends_down[b])
                def _(i=i, b=b):
                    y_copy(i, b).start()

        if i <= cb:
            @pl.when(r != 0)
            def _(i=i):
                z_copy(i).wait_recv()

            @pl.when(r < row_count - 1)
            def _(i=i):
                z_copy(i).start()

    def spread(p):
        for col in reversed(range(1, col_count)):
            w_col(p, col).start()

    @pl.when(root)
    def _():
        lane = lax.broadcasted_iota(jnp.int32, (half, nb), 1)
        sub = lax.broadcasted_iota(jnp.int32, (half, nb), 0)
        right = jnp.where(lane == sub + half, 1.0, 0.0).astype(F32)
        up, inv = eliminate(groups(ybuf[0, 0:half, :]), groups(right))
        wbuf[0] = pltpu.roll(inv, half, 1)
        ubuf[0] = up
        for row in reversed(range(1, row_count)):
            w_row(0, row).start()
        spread(0)
        up12 = pltpu.roll(up, half, 1)
        beside = jnp.where(lane < half, up12, inv)
        change = dot(up12, beside, ((0,), (0,)))[0:half, :]
        low_rows = pltpu.roll(ybuf[0, half:nb, :], half, 1)
        start = jnp.where(lane < half, low_rows, 0.0) - change
        up, inv = eliminate(groups(start), groups(right))
        wbuf[1] = jnp.where(lane < half, pltpu.roll(up, half, 1), inv)
        ubuf[1] = jnp.where(lane < half, 0.0, pltpu.roll(up, half, 1))
        for row in reversed(range(1, row_count)):
            w_row(1, row).start()
        spread(1)

    @pl.when((c == 0) & (r != 0))
    def _():
        for p in range(2):
            w_row(p, 0).wait_recv()
            spread(p)

    @pl.when(c != 0)
    def _():
        for p in range(2):
            w_col(p, 0).wait_recv()

    w = wbuf[...].reshape(nb, nb)
    own = dot(ybuf[...].reshape(rb * nb, nb), w, ((1,), (1,)))
    lead = dot(tbuf[...], w, ((1,), (1,)))
    reduced = dot(lead, own, ((1,), (1,)))
    for i in range(rb):
        flat = b_ref[pl.ds(i, sides, stride=rb), :] - reduced[:, i * nb : (i + 1) * nb]
        if i == 0:
            flat = jnp.where(r == 0, lead, flat)
        red_ref[pl.ds(i, sides, stride=rb), :] = flat
    for j in range(cb):
        across = dot(w, zbuf[j], ((1,), (0,)))
        change = dot(own, across, ((1,), (0,)))
        for i in range(rb):
            here = pl.ds(i * nb * cb + j, nb, stride=cb)
            block = a_ref[here, :] - change[i * nb : (i + 1) * nb]
            if i == 0:
                block = jnp.where(r == 0, 0.0, block)
            if j == 0:
                block = jnp.where(c == 0, own[i * nb : (i + 1) * nb], block)
            out_ref[here, :] = block

    @pl.when(root)
    def _():
        lane = lax.broadcasted_iota(jnp.int32, (nb, nb), 1)
        sub = lax.broadcasted_iota(jnp.int32, (nb, nb), 0)
        low = jnp.transpose(ubuf[...].reshape(nb, nb))
        out_ref[pl.ds(0, nb, stride=cb), :] = jnp.where(sub >= lane, low, 0.0)

    for i in range(rb):
        for b in range(bits):
            @pl.when(sends_down[b])
            def _(i=i, b=b):
                y_copy(i, b).wait_send()

    @pl.when(r < row_count - 1)
    def _():
        for j in range(cb + 1):
            z_copy(j).wait_send()

    @pl.when(root)
    def _():
        for row in range(1, row_count):
            for p in range(2):
                w_row(p, row).wait_send()

    @pl.when(c == 0)
    def _():
        for col in range(1, col_count):
            for p in range(2):
                w_col(p, col).wait_send()


def on_device(row_count, col_count, normal_matrix, right_sides):
    rb, _, nb, cb, _, _ = normal_matrix.shape
    sides = right_sides.shape[0]
    bits = max(1, (col_count - 1).bit_length())
    sizes = (row_count, col_count, rb, cb, nb, sides)
    dma = pltpu.SemaphoreType.DMA
    out, red = pl.pallas_call(
        functools.partial(kernel, sizes),
        out_shape=(
            jax.ShapeDtypeStruct((rb * nb * cb, nb), F32),
            jax.ShapeDtypeStruct((sides * rb, nb), F32),
        ),
        in_specs=[pl.BlockSpec(memory_space=pltpu.VMEM)] * 2,
        out_specs=[pl.BlockSpec(memory_space=pltpu.VMEM)] * 2,
        scratch_shapes=[
            pltpu.VMEM((rb, nb, nb), F32),
            pltpu.VMEM((cb, nb, nb), F32),
            pltpu.VMEM((sides, nb), F32),
            pltpu.VMEM((2, nb // 2, nb), F32),
            pltpu.VMEM((2, nb // 2, nb), F32),
            dma((bits, rb)),
            dma((rb,)),
            dma((cb + 1,)),
            dma((cb + 1,)),
            dma((row_count, 2)),
            dma((col_count, 2)),
            dma((2,)),
        ],
        compiler_params=pltpu.CompilerParams(
            collective_id=0, has_side_effects=True, vmem_limit_bytes=32 * 1024 * 1024
        ),
    )(normal_matrix.reshape(rb * nb * cb, nb), right_sides.reshape(sides * rb, nb))
    return out.reshape(normal_matrix.shape), red.reshape(right_sides.shape)


def solution(mesh):
    placed = (P(None, "row", None, None, "col", None), P("col", None, "row", None))
    return jax.shard_map(
        functools.partial(on_device, mesh.shape["row"], mesh.shape["col"]),
        mesh=mesh,
        in_specs=placed,
        out_specs=placed,
        check_vma=False,
    )
```

time: 183 us -> 29.1 us (0.16)
  the two profiles are of different devices: /device:TPU:0 before, /device:TPU:31 now
where the time goes in v1:
time: 29.1 us; the launch traced here: 28.9 us
  Pallas kernels  25.1 us (86%)
  local copies, waits for them, and re-layouts  3.15 us (11%)
  between operations  0.65 us (2%)
    pallas_call x1, Pallas kernels, on_device(): pl.pallas_call(functools.partial(kernel, sizes), out_shape=(jax.ShapeDtyp...  25.1 us
    unnamed x6, local copies, waits for them, and re-layouts  3.15 us

profile of v1, /device:TPU:31, one launch (start us, length us, event | category | flops | bytes accessed | tf_op | source)
XLA Modules:
  0.0 28.9 jit_solution(6310081319720104300)
XLA Ops:
  0.6 0.0 copy-start
  0.6 1.0 %copy-done = f32[4,1,128,2,1,128]{5,4,3,2,1,0:T(1,128)S(1)} copy-done((f32[4,1,128,2,1,128]{5,4,3,2,1,0:T(1,128)S(1)}, f32[4,1,128,2,1,128]{5,4,3,2,1,0:T(1,128)}, u32[]{:S(2)}) %copy-start) | copy-done | bytes 524312
  1.7 0.0 copy-start.1
  1.7 0.7 %copy-done.1 = f32[8,4,1,128]{3,2,1,0:T(1,128)S(1)} copy-done((f32[8,4,1,128]{3,2,1,0:T(1,128)S(1)}, f32[8,4,1,128]{3,2,1,0:T(1,128)}, u32[]{:S(2)}) %copy-start.1) | copy-done | bytes 16408
  2.4 25.1 %shard_map.41 = (f32[1024,128]{1,0:T(8,128)S(1)}, f32[32,128]{1,0:T(8,128)S(1)}) custom-call(f32[1024,128]{1,0:T(8,128)S(1)} %bitcast.8, f32[32,128]{1,0:T(8,128)S(1)} %bitcast.10), custom_call_target="tpu_custom_call" | custom-call | tf_op jit(solution)/shard_map/pallas_call | solution.py:263
  27.4 0.8 %copy.8 = f32[4,1,128,2,1,128]{5,4,3,2,1,0:T(1,128)} copy(f32[4,1,128,2,1,128]{5,4,3,2,1,0:T(1,128)S(1)} %bitcast.9) | data formatting | bytes 1048576
  28.2 0.6 %copy.9 = f32[8,4,1,128]{3,2,1,0:T(1,128)} copy(f32[8,4,1,128]{3,2,1,0:T(1,128)S(1)} %bitcast.11) | data formatting | bytes 32768
Async XLA Ops:
  0.6 1.0 %copy-start = (f32[4,1,128,2,1,128]{5,4,3,2,1,0:T(1,128)S(1)}, f32[4,1,128,2,1,128]{5,4,3,2,1,0:T(1,128)}, u32[]{:S(2)}) copy-start(f32[4,1,128,2,1,128]{5,4,3,2,1,0:T(1,128)} %param.2) | copy-start | bytes 1572868
  1.7 0.7 %copy-start.1 = (f32[8,4,1,128]{3,2,1,0:T(1,128)S(1)}, f32[8,4,1,128]{3,2,1,0:T(1,128)}, u32[]{:S(2)}) copy-start(f32[8,4,1,128]{3,2,1,0:T(1,128)} %param.3) | copy-start | bytes 49156

commit v2 on v1

--- a/solution.py
+++ b/solution.py
@@ -63,12 +63,13 @@
 
 
 def kernel(
-    sizes, a_ref, b_ref, out_ref, red_ref,
-    ybuf, zbuf, tbuf, wbuf, ubuf,
+    sizes, a_hbm, b_hbm, out_ref, red_ref,
+    a_ref, b_ref, load, ybuf, zbuf, tbuf, wbuf, ubuf,
     ysend, yrecv, zsend, zrecv, wrow, wcol, wrecv,
 ):
     row_count, col_count, rb, cb, nb, sides = sizes
     half = nb // 2
+    pieces = 2 * cb + 1
     r = lax.axis_index("row")
     c = lax.axis_index("col")
     bits = max(1, (col_count - 1).bit_length())
@@ -80,16 +81,12 @@
     for b in range(bits):
         parent = jnp.where(lax.rem(c, 2 ** (b + 1)) == 2**b, c - 2**b, parent)
 
-    @pl.when(c == 0)
-    def _():
-        for i in range(rb):
-            ybuf[i] = a_ref[pl.ds(i * nb * cb, nb, stride=cb), :]
-
-    @pl.when(r == 0)
-    def _():
-        for j in range(cb):
-            zbuf[j] = a_ref[pl.ds(j, nb, stride=cb), :]
-        tbuf[...] = b_ref[pl.ds(0, sides, stride=rb), :]
+    loads = (
+        pltpu.make_async_copy(a_hbm, a_ref, load.at[0]),
+        pltpu.make_async_copy(b_hbm, b_ref, load.at[1]),
+    )
+    for one in loads:
+        one.start()
 
     barrier = pltpu.get_barrier_semaphore()
 
@@ -110,6 +107,20 @@
     @pl.when((r != 0) & (c == 0))
     def _():
         greet(0, 0)
+
+    for one in loads:
+        one.wait()
+
+    @pl.when(c == 0)
+    def _():
+        for i in range(rb):
+            ybuf[i] = a_ref[pl.ds(i * nb * cb, nb, stride=cb), :]
+
+    @pl.when(r == 0)
+    def _():
+        for j in range(cb):
+            zbuf[j] = a_ref[pl.ds(j, nb, stride=cb), :]
+        tbuf[...] = b_ref[pl.ds(0, sides, stride=rb), :]
 
     targets = jnp.where(r < row_count - 1, 1, 0)
     for b in range(bits):
@@ -135,7 +146,7 @@
         return copy(ybuf.at[i], ysend.at[b, i], yrecv.at[i], r, c + 2**b)
 
     def z_copy(j):
-        ref = zbuf.at[j] if j < cb else tbuf
+        ref = zbuf.at[j // 2, pl.ds(j % 2 * half, half)] if j < 2 * cb else tbuf
         return copy(ref, zsend.at[j], zrecv.at[j], r + 1, c)
 
     def w_row(p, row):
@@ -144,25 +155,45 @@
     def w_col(p, col):
         return copy(wbuf.at[p], wcol.at[col, p], wrecv.at[p], r, col)
 
-    for i in range(max(rb, cb + 1)):
-        if i < rb:
-            @pl.when(c != 0)
-            def _(i=i):
-                y_copy(i, 0).wait_recv()
-
+    @pl.when(c == 0)
+    def _():
+        for i in range(rb):
             for b in reversed(range(bits)):
                 @pl.when(sends_down[b])
                 def _(i=i, b=b):
                     y_copy(i, b).start()
 
-        if i <= cb:
-            @pl.when(r != 0)
-            def _(i=i):
-                z_copy(i).wait_recv()
-
-            @pl.when(r < row_count - 1)
-            def _(i=i):
-                z_copy(i).start()
+    @pl.when(r == 0)
+    def _():
+        for j in range(pieces):
+            z_copy(j).start()
+
+    relays = (r != 0) & (r < row_count - 1)
+    inner = (c != 0) & (lax.rem(c, 2) == 0)
+
+    def relay(j):
+        z_copy(j).wait_recv()
+        z_copy(j).start()
+
+    @pl.when(relays & ~inner)
+    def _():
+        for j in range(pieces):
+            relay(j)
+
+    @pl.when(inner)
+    def _():
+        for i in range(max(rb, pieces)):
+            if i < rb:
+                y_copy(i, 0).wait_recv()
+                for b in reversed(range(bits)):
+                    @pl.when(sends_down[b])
+                    def _(i=i, b=b):
+                        y_copy(i, b).start()
+
+            if i < pieces:
+                @pl.when(relays)
+                def _(i=i):
+                    relay(i)
 
     def spread(p):
         for col in reversed(range(1, col_count)):
@@ -202,6 +233,16 @@
         for p in range(2):
             w_col(p, 0).wait_recv()
 
+    @pl.when((c != 0) & ~inner)
+    def _():
+        for i in range(rb):
+            y_copy(i, 0).wait_recv()
+
+    @pl.when((r != 0) & ~relays)
+    def _():
+        for j in range(pieces):
+            z_copy(j).wait_recv()
+
     w = wbuf[...].reshape(nb, nb)
     own = dot(ybuf[...].reshape(rb * nb, nb), w, ((1,), (1,)))
     lead = dot(tbuf[...], w, ((1,), (1,)))
@@ -238,7 +279,7 @@
 
     @pl.when(r < row_count - 1)
     def _():
-        for j in range(cb + 1):
+        for j in range(pieces):
             z_copy(j).wait_send()
 
     @pl.when(root)
@@ -266,9 +307,12 @@
             jax.ShapeDtypeStruct((rb * nb * cb, nb), F32),
             jax.ShapeDtypeStruct((sides * rb, nb), F32),
         ),
-        in_specs=[pl.BlockSpec(memory_space=pltpu.VMEM)] * 2,
+        in_specs=[pl.BlockSpec(memory_space=pl.ANY)] * 2,
         out_specs=[pl.BlockSpec(memory_space=pltpu.VMEM)] * 2,
         scratch_shapes=[
+            pltpu.VMEM((rb * nb * cb, nb), F32),
+            pltpu.VMEM((sides * rb, nb), F32),
+            dma((2,)),
             pltpu.VMEM((rb, nb, nb), F32),
             pltpu.VMEM((cb, nb, nb), F32),
             pltpu.VMEM((sides, nb), F32),
@@ -276,14 +320,14 @@
             pltpu.VMEM((2, nb // 2, nb), F32),
             dma((bits, rb)),
             dma((rb,)),
-            dma((cb + 1,)),
-            dma((cb + 1,)),
+            dma((2 * cb + 1,)),
+            dma((2 * cb + 1,)),
             dma((row_count, 2)),
             dma((col_count, 2)),
             dma((2,)),
         ],
         compiler_params=pltpu.CompilerParams(
-            collective_id=0, has_side_effects=True, vmem_limit_bytes=32 * 1024 * 1024
+            collective_id=0, has_side_effects=True, vmem_limit_bytes=56 * 1024 * 1024
         ),
     )(normal_matrix.reshape(rb * nb * cb, nb), right_sides.reshape(sides * rb, nb))
     return out.reshape(normal_matrix.shape), red.reshape(right_sides.shape)

time: 29.1 us -> 21.2 us (0.73)
  the two profiles are of different devices: /device:TPU:31 before, /device:TPU:30 now
where the time goes in v2:
time: 21.2 us; the launch traced here: 21.1 us
  Pallas kernels  17.6 us (83%)
  local copies, waits for them, and re-layouts  2.81 us (13%)
  between operations  0.65 us (3%)
    pallas_call x1, Pallas kernels, on_device(): pl.pallas_call(functools.partial(kernel, sizes), out_shape=(jax.ShapeDtyp...  17.6 us
    unnamed x4, local copies, waits for them, and re-layouts  2.81 us

profile of v2, /device:TPU:30, one launch (start us, length us, event | category | flops | bytes accessed | tf_op | source)
XLA Modules:
  0.0 21.1 jit_solution(14576791666174267576)
XLA Ops:
  0.6 17.6 %shard_map.41 = (f32[1024,128]{1,0:T(8,128)}, f32[32,128]{1,0:T(8,128)}) custom-call(f32[1024,128]{1,0:T(8,128)} %bitcast.8, f32[32,128]{1,0:T(8,128)} %bitcast.10), custom_call_target="tpu_custom_call" | custom-call | tf_op jit(solution)/shard_map/pallas_call | solution.py:304
  18.3 0.0 copy-start
  18.3 2.2 %copy.8 = f32[4,1,128,2,1,128]{5,4,3,2,1,0:T(1,128)} copy(f32[4,1,128,2,1,128]{5,4,3,2,1,0:T(1,128)} %bitcast.9) | data formatting | bytes 1048576
  20.5 0.0 copy-done
  20.5 0.6 %copy.9 = f32[8,4,1,128]{3,2,1,0:T(1,128)} copy(f32[8,4,1,128]{3,2,1,0:T(1,128)S(1)} %bitcast.11) | data formatting | bytes 32768
Async XLA Ops:
  18.3 2.2 %copy-start = (f32[32,128]{1,0:T(8,128)S(1)}, f32[32,128]{1,0:T(8,128)}, u32[]{:S(2)}) copy-start(f32[32,128]{1,0:T(8,128)} %get-tuple-element.5) | copy-start | bytes 49156

commit v3 on v2

--- a/solution.py
+++ b/solution.py
@@ -62,9 +62,31 @@
     return [x[8 * t : 8 * t + 8] for t in range(x.shape[0] // 8)]
 
 
+def tree(count):
+    children = [[] for _ in range(count)]
+    into = {0: 0}
+    for chip in range(1, (count + 1) // 2):
+        high = 1 << (chip.bit_length() - 1)
+        source = chip - high
+        into[chip] = into[source] if source else (chip.bit_length() - 1) % 2
+        children[2 * source + into[chip]].append(2 * chip + into[chip])
+    for chip in range((count + 1) // 2):
+        if 2 * chip + 1 < count:
+            children[2 * chip + into[chip]].append(2 * chip + 1 - into[chip])
+    return children
+
+
+def pick(table, index):
+    value = index * 0
+    for at, entry in enumerate(table):
+        if entry:
+            value = jnp.where(index == at, entry, value)
+    return value
+
+
 def kernel(
     sizes, a_hbm, b_hbm, out_ref, red_ref,
-    a_ref, b_ref, load, ybuf, zbuf, tbuf, wbuf, ubuf,
+    a_ref, b_ref, load, ybuf, zbuf, tbuf, wbuf, ubuf, rest,
     ysend, yrecv, zsend, zrecv, wrow, wcol, wrecv,
 ):
     row_count, col_count, rb, cb, nb, sides = sizes
@@ -72,15 +94,15 @@
     pieces = 2 * cb + 1
     r = lax.axis_index("row")
     c = lax.axis_index("col")
-    bits = max(1, (col_count - 1).bit_length())
+    children = tree(col_count)
+    slots = max(len(x) for x in children)
+    child = [pick([x[k] if k < len(x) else 0 for x in children], c) for k in range(slots)]
+    parents = [0] * col_count
+    for at, kids in enumerate(children):
+        for kid in kids:
+            parents[kid] = at
+    parent = pick(parents, c)
     root = (r == 0) & (c == 0)
-    sends_down = [
-        (lax.rem(c, 2 ** (b + 1)) == 0) & (c + 2**b < col_count) for b in range(bits)
-    ]
-    parent = c * 0
-    for b in range(bits):
-        parent = jnp.where(lax.rem(c, 2 ** (b + 1)) == 2**b, c - 2**b, parent)
-
     loads = (
         pltpu.make_async_copy(a_hbm, a_ref, load.at[0]),
         pltpu.make_async_copy(b_hbm, b_ref, load.at[1]),
@@ -122,9 +144,24 @@
             zbuf[j] = a_ref[pl.ds(j, nb, stride=cb), :]
         tbuf[...] = b_ref[pl.ds(0, sides, stride=rb), :]
 
+    lane = lax.broadcasted_iota(jnp.int32, (half, nb), 1)
+    sub = lax.broadcasted_iota(jnp.int32, (half, nb), 0)
+    right = jnp.where(lane == sub + half, 1.0, 0.0).astype(F32)
+
+    @pl.when(root)
+    def _():
+        up, inv = eliminate(groups(ybuf[0, 0:half, :]), groups(right))
+        wbuf[0] = pltpu.roll(inv, half, 1)
+        ubuf[0] = up
+        up12 = pltpu.roll(up, half, 1)
+        beside = jnp.where(lane < half, up12, inv)
+        change = dot(up12, beside, ((0,), (0,)))[0:half, :]
+        low_rows = pltpu.roll(ybuf[0, half:nb, :], half, 1)
+        rest[...] = jnp.where(lane < half, low_rows, 0.0) - change
+
     targets = jnp.where(r < row_count - 1, 1, 0)
-    for b in range(bits):
-        targets = targets + jnp.where(sends_down[b], 1, 0)
+    for k in range(slots):
+        targets = targets + jnp.where(child[k] != 0, 1, 0)
     targets = targets + jnp.where(c == 0, col_count - 1, 0)
     targets = targets + jnp.where(root, row_count - 1, 0)
 
@@ -142,8 +179,8 @@
             device_id_type=pl.DeviceIdType.MESH,
         )
 
-    def y_copy(i, b):
-        return copy(ybuf.at[i], ysend.at[b, i], yrecv.at[i], r, c + 2**b)
+    def y_copy(i, k):
+        return copy(ybuf.at[i], ysend.at[k, i], yrecv.at[i], r, child[k])
 
     def z_copy(j):
         ref = zbuf.at[j // 2, pl.ds(j % 2 * half, half)] if j < 2 * cb else tbuf
@@ -155,21 +192,21 @@
     def w_col(p, col):
         return copy(wbuf.at[p], wcol.at[col, p], wrecv.at[p], r, col)
 
+    @pl.when(r == 0)
+    def _():
+        for j in range(pieces):
+            z_copy(j).start()
+
     @pl.when(c == 0)
     def _():
         for i in range(rb):
-            for b in reversed(range(bits)):
-                @pl.when(sends_down[b])
+            for b in range(slots):
+                @pl.when(child[b] != 0)
                 def _(i=i, b=b):
                     y_copy(i, b).start()
 
-    @pl.when(r == 0)
-    def _():
-        for j in range(pieces):
-            z_copy(j).start()
-
     relays = (r != 0) & (r < row_count - 1)
-    inner = (c != 0) & (lax.rem(c, 2) == 0)
+    inner = (c != 0) & (child[0] != 0)
 
     def relay(j):
         z_copy(j).wait_recv()
@@ -185,8 +222,8 @@
         for i in range(max(rb, pieces)):
             if i < rb:
                 y_copy(i, 0).wait_recv()
-                for b in reversed(range(bits)):
-                    @pl.when(sends_down[b])
+                for b in range(slots):
+                    @pl.when(child[b] != 0)
                     def _(i=i, b=b):
                         y_copy(i, b).start()
 
@@ -201,26 +238,15 @@
 
     @pl.when(root)
     def _():
-        lane = lax.broadcasted_iota(jnp.int32, (half, nb), 1)
-        sub = lax.broadcasted_iota(jnp.int32, (half, nb), 0)
-        right = jnp.where(lane == sub + half, 1.0, 0.0).astype(F32)
-        up, inv = eliminate(groups(ybuf[0, 0:half, :]), groups(right))
-        wbuf[0] = pltpu.roll(inv, half, 1)
-        ubuf[0] = up
         for row in reversed(range(1, row_count)):
             w_row(0, row).start()
         spread(0)
-        up12 = pltpu.roll(up, half, 1)
-        beside = jnp.where(lane < half, up12, inv)
-        change = dot(up12, beside, ((0,), (0,)))[0:half, :]
-        low_rows = pltpu.roll(ybuf[0, half:nb, :], half, 1)
-        start = jnp.where(lane < half, low_rows, 0.0) - change
-        up, inv = eliminate(groups(start), groups(right))
+        up, inv = eliminate(groups(rest[...]), groups(right))
         wbuf[1] = jnp.where(lane < half, pltpu.roll(up, half, 1), inv)
-        ubuf[1] = jnp.where(lane < half, 0.0, pltpu.roll(up, half, 1))
         for row in reversed(range(1, row_count)):
             w_row(1, row).start()
         spread(1)
+        ubuf[1] = jnp.where(lane < half, 0.0, pltpu.roll(up, half, 1))
 
     @pl.when((c == 0) & (r != 0))
     def _():
@@ -272,8 +298,8 @@
         out_ref[pl.ds(0, nb, stride=cb), :] = jnp.where(sub >= lane, low, 0.0)
 
     for i in range(rb):
-        for b in range(bits):
-            @pl.when(sends_down[b])
+        for b in range(slots):
+            @pl.when(child[b] != 0)
             def _(i=i, b=b):
                 y_copy(i, b).wait_send()
 
@@ -298,7 +324,7 @@
 def on_device(row_count, col_count, normal_matrix, right_sides):
     rb, _, nb, cb, _, _ = normal_matrix.shape
     sides = right_sides.shape[0]
-    bits = max(1, (col_count - 1).bit_length())
+    slots = max(len(x) for x in tree(col_count))
     sizes = (row_count, col_count, rb, cb, nb, sides)
     dma = pltpu.SemaphoreType.DMA
     out, red = pl.pallas_call(
@@ -318,7 +344,8 @@
             pltpu.VMEM((sides, nb), F32),
             pltpu.VMEM((2, nb // 2, nb), F32),
             pltpu.VMEM((2, nb // 2, nb), F32),
-            dma((bits, rb)),
+            pltpu.VMEM((nb // 2, nb), F32),
+            dma((slots, rb)),
             dma((rb,)),
             dma((2 * cb + 1,)),
             dma((2 * cb + 1,)),
@@ -327,7 +354,7 @@
             dma((2,)),
         ],
         compiler_params=pltpu.CompilerParams(
-            collective_id=0, has_side_effects=True, vmem_limit_bytes=56 * 1024 * 1024
+            collective_id=0, has_side_effects=True, vmem_limit_bytes=53 * 1024 * 1024 + 128 * 1024
         ),
     )(normal_matrix.reshape(rb * nb * cb, nb), right_sides.reshape(sides * rb, nb))
     return out.reshape(normal_matrix.shape), red.reshape(right_sides.shape)

time: 21.2 us -> 19.9 us (0.939)
  the two profiles are of different devices: /device:TPU:30 before, /device:TPU:18 now
where the time goes in v3:
time: 19.9 us; the launch traced here: 19.6 us
  Pallas kernels  16.9 us (85%)
  local copies, waits for them, and re-layouts  2.11 us (11%)
  between operations  0.65 us (3%)
    pallas_call x1, Pallas kernels, on_device(): pl.pallas_call(functools.partial(kernel, sizes), out_shape=(jax.ShapeDtyp...  16.9 us
    unnamed x4, local copies, waits for them, and re-layouts  2.11 us

profile of v3, /device:TPU:18, one launch (start us, length us, event | category | flops | bytes accessed | tf_op | source)
XLA Modules:
  0.0 19.6 jit_solution(12557340292415304340)
XLA Ops:
  0.6 0.0 copy-start
  0.6 0.7 %copy-done = f32[8,4,1,128]{3,2,1,0:T(1,128)S(1)} copy-done((f32[8,4,1,128]{3,2,1,0:T(1,128)S(1)}, f32[8,4,1,128]{3,2,1,0:T(1,128)}, u32[]{:S(2)}) %copy-start) | copy-done | bytes 16408
  1.3 16.9 %shard_map.41 = (f32[1024,128]{1,0:T(8,128)S(1)}, f32[32,128]{1,0:T(8,128)S(1)}) custom-call(f32[1024,128]{1,0:T(8,128)} %bitcast.11, f32[32,128]{1,0:T(8,128)S(1)} %bitcast.9), custom_call_target="tpu_custom_call" | custom-call | tf_op jit(solution)/shard_map/pallas_call | solution.py:330
  18.2 0.8 %copy.8 = f32[4,1,128,2,1,128]{5,4,3,2,1,0:T(1,128)} copy(f32[4,1,128,2,1,128]{5,4,3,2,1,0:T(1,128)S(1)} %bitcast.8) | data formatting | bytes 1048576
  19.0 0.6 %copy.9 = f32[8,4,1,128]{3,2,1,0:T(1,128)} copy(f32[8,4,1,128]{3,2,1,0:T(1,128)S(1)} %bitcast.10) | data formatting | bytes 32768
Async XLA Ops:
  0.6 0.7 %copy-start = (f32[8,4,1,128]{3,2,1,0:T(1,128)S(1)}, f32[8,4,1,128]{3,2,1,0:T(1,128)}, u32[]{:S(2)}) copy-start(f32[8,4,1,128]{3,2,1,0:T(1,128)} %param.3) | copy-start | bytes 49156

commit v4 on v3

--- a/solution.py
+++ b/solution.py
@@ -16,7 +16,7 @@
     )
 
 
-def eliminate(first, second):
+def eliminate(first, second, early=None):
     count = len(first)
     shape = first[0].shape
     sub = lax.broadcasted_iota(jnp.int32, shape, 0)
@@ -55,6 +55,8 @@
             done1 = jnp.where(sub == k, rows1[k], done1)
             done2 = jnp.where(sub == k, rows2[k], done2)
         first[b], second[b] = done1, done2
+        if early is not None and b == count // 2 - 1:
+            early(jnp.concatenate(first[: b + 1], axis=0), jnp.concatenate(second[: b + 1], axis=0))
     return jnp.concatenate(first, axis=0), jnp.concatenate(second, axis=0)
 
 
@@ -62,17 +64,25 @@
     return [x[8 * t : 8 * t + 8] for t in range(x.shape[0] // 8)]
 
 
+def leader(chip):
+    return (chip.bit_length() - 1) % 2 if chip and chip & (chip - 1) == 0 else 0
+
+
 def tree(count):
     children = [[] for _ in range(count)]
-    into = {0: 0}
     for chip in range(1, (count + 1) // 2):
         high = 1 << (chip.bit_length() - 1)
-        source = chip - high
-        into[chip] = into[source] if source else (chip.bit_length() - 1) % 2
-        children[2 * source + into[chip]].append(2 * chip + into[chip])
+        low = chip & -chip
+        if high == low:
+            first = leader(chip)
+            children[first].append(2 * chip + first)
+        else:
+            children[2 * (chip - high)].append(2 * chip)
+            children[2 * (chip - low) + 1].append(2 * chip + 1)
     for chip in range((count + 1) // 2):
-        if 2 * chip + 1 < count:
-            children[2 * chip + into[chip]].append(2 * chip + 1 - into[chip])
+        if chip & (chip - 1) == 0:
+            first = leader(chip)
+            children[2 * chip + first].append(2 * chip + 1 - first)
     return children
 
 
@@ -80,18 +90,19 @@
     value = index * 0
     for at, entry in enumerate(table):
         if entry:
-            value = jnp.where(index == at, entry, value)
+            value = jnp.where(index == at, int(entry), value)
     return value
 
 
 def kernel(
     sizes, a_hbm, b_hbm, out_ref, red_ref,
     a_ref, b_ref, load, ybuf, zbuf, tbuf, wbuf, ubuf, rest,
-    ysend, yrecv, zsend, zrecv, wrow, wcol, wrecv,
+    ysend, yrecv, zsend, zrecv, wrow, wcol, wpass, wrecv,
 ):
     row_count, col_count, rb, cb, nb, sides = sizes
     half = nb // 2
     pieces = 2 * cb + 1
+    parts = ((0, half), (half, half // 2), (half + half // 2, half // 2))
     r = lax.axis_index("row")
     c = lax.axis_index("col")
     children = tree(col_count)
@@ -102,6 +113,9 @@
         for kid in kids:
             parents[kid] = at
     parent = pick(parents, c)
+    heads = [2 * h + leader(h) for h in range(col_count // 2)]
+    partner = c + 1 - 2 * lax.rem(c, 2)
+    leads = pick([at in heads for at in range(col_count)], c) == 1
     root = (r == 0) & (c == 0)
     loads = (
         pltpu.make_async_copy(a_hbm, a_ref, load.at[0]),
@@ -120,7 +134,7 @@
     @pl.when(c != 0)
     def _():
         greet(r, parent)
-        greet(r, 0)
+        greet(r, jnp.where(leads, 0, partner))
 
     @pl.when(r != 0)
     def _():
@@ -151,7 +165,7 @@
     @pl.when(root)
     def _():
         up, inv = eliminate(groups(ybuf[0, 0:half, :]), groups(right))
-        wbuf[0] = pltpu.roll(inv, half, 1)
+        wbuf[pl.ds(*parts[0])] = pltpu.roll(inv, half, 1)
         ubuf[0] = up
         up12 = pltpu.roll(up, half, 1)
         beside = jnp.where(lane < half, up12, inv)
@@ -162,7 +176,7 @@
     targets = jnp.where(r < row_count - 1, 1, 0)
     for k in range(slots):
         targets = targets + jnp.where(child[k] != 0, 1, 0)
-    targets = targets + jnp.where(c == 0, col_count - 1, 0)
+    targets = targets + jnp.where(c == 0, len(heads) - 1, 0) + jnp.where(leads, 1, 0)
     targets = targets + jnp.where(root, row_count - 1, 0)
 
     @pl.when(targets > 0)
@@ -186,11 +200,17 @@
         ref = zbuf.at[j // 2, pl.ds(j % 2 * half, half)] if j < 2 * cb else tbuf
         return copy(ref, zsend.at[j], zrecv.at[j], r + 1, c)
 
+    def w_part(p):
+        return wbuf.at[pl.ds(*parts[p])]
+
     def w_row(p, row):
-        return copy(wbuf.at[p], wrow.at[row, p], wrecv.at[p], row, 0)
-
-    def w_col(p, col):
-        return copy(wbuf.at[p], wcol.at[col, p], wrecv.at[p], r, col)
+        return copy(w_part(p), wrow.at[row, p], wrecv.at[p], row, 0)
+
+    def w_col(p, head):
+        return copy(w_part(p), wcol.at[head, p], wrecv.at[p], r, heads[head])
+
+    def w_pass(p):
+        return copy(w_part(p), wpass.at[p], wrecv.at[p], r, partner)
 
     @pl.when(r == 0)
     def _():
@@ -233,31 +253,48 @@
                     relay(i)
 
     def spread(p):
-        for col in reversed(range(1, col_count)):
-            w_col(p, col).start()
+        for head in reversed(range(1, len(heads))):
+            w_col(p, head).start()
+        w_pass(p).start()
+
+    def send(p):
+        for row in reversed(range(1, row_count)):
+            w_row(p, row).start()
+        spread(p)
+
+    def inverse_rows(up, inv):
+        wide = lax.broadcasted_iota(jnp.int32, up.shape, 1)
+        return jnp.where(wide < half, pltpu.roll(up, half, 1), inv)
 
     @pl.when(root)
     def _():
-        for row in reversed(range(1, row_count)):
-            w_row(0, row).start()
-        spread(0)
-        up, inv = eliminate(groups(rest[...]), groups(right))
-        wbuf[1] = jnp.where(lane < half, pltpu.roll(up, half, 1), inv)
-        for row in reversed(range(1, row_count)):
-            w_row(1, row).start()
-        spread(1)
+        send(0)
+
+        def early(up, inv):
+            wbuf[pl.ds(*parts[1])] = inverse_rows(up, inv)
+            send(1)
+
+        up, inv = eliminate(groups(rest[...]), groups(right), early)
+        wbuf[pl.ds(*parts[2])] = inverse_rows(up, inv)[half // 2 :]
+        send(2)
         ubuf[1] = jnp.where(lane < half, 0.0, pltpu.roll(up, half, 1))
 
     @pl.when((c == 0) & (r != 0))
     def _():
-        for p in range(2):
+        for p in range(3):
             w_row(p, 0).wait_recv()
             spread(p)
 
-    @pl.when(c != 0)
-    def _():
-        for p in range(2):
-            w_col(p, 0).wait_recv()
+    @pl.when((c != 0) & leads)
+    def _():
+        for p in range(3):
+            w_pass(p).wait_recv()
+            w_pass(p).start()
+
+    @pl.when(~leads)
+    def _():
+        for p in range(3):
+            w_pass(p).wait_recv()
 
     @pl.when((c != 0) & ~inner)
     def _():
@@ -269,7 +306,7 @@
         for j in range(pieces):
             z_copy(j).wait_recv()
 
-    w = wbuf[...].reshape(nb, nb)
+    w = wbuf[...]
     own = dot(ybuf[...].reshape(rb * nb, nb), w, ((1,), (1,)))
     lead = dot(tbuf[...], w, ((1,), (1,)))
     reduced = dot(lead, own, ((1,), (1,)))
@@ -311,14 +348,19 @@
     @pl.when(root)
     def _():
         for row in range(1, row_count):
-            for p in range(2):
+            for p in range(3):
                 w_row(p, row).wait_send()
 
     @pl.when(c == 0)
     def _():
-        for col in range(1, col_count):
-            for p in range(2):
-                w_col(p, col).wait_send()
+        for head in range(1, len(heads)):
+            for p in range(3):
+                w_col(p, head).wait_send()
+
+    @pl.when(leads)
+    def _():
+        for p in range(3):
+            w_pass(p).wait_send()
 
 
 def on_device(row_count, col_count, normal_matrix, right_sides):
@@ -342,16 +384,17 @@
             pltpu.VMEM((rb, nb, nb), F32),
             pltpu.VMEM((cb, nb, nb), F32),
             pltpu.VMEM((sides, nb), F32),
-            pltpu.VMEM((2, nb // 2, nb), F32),
+            pltpu.VMEM((nb, nb), F32),
             pltpu.VMEM((2, nb // 2, nb), F32),
             pltpu.VMEM((nb // 2, nb), F32),
             dma((slots, rb)),
             dma((rb,)),
             dma((2 * cb + 1,)),
             dma((2 * cb + 1,)),
-            dma((row_count, 2)),
-            dma((col_count, 2)),
-            dma((2,)),
+            dma((row_count, 3)),
+            dma((col_count // 2, 3)),
+            dma((3,)),
+            dma((3,)),
         ],
         compiler_params=pltpu.CompilerParams(
             collective_id=0, has_side_effects=True, vmem_limit_bytes=53 * 1024 * 1024 + 128 * 1024

time: 19.9 us -> 19.9 us (level)
  the two profiles are of different devices: /device:TPU:18 before, /device:TPU:19 now
where the time goes in v4:
time: 19.9 us; the launch traced here: 19.6 us
  Pallas kernels  16.9 us (85%)
  local copies, waits for them, and re-layouts  2.11 us (11%)
  between operations  0.65 us (3%)
    pallas_call x1, Pallas kernels, on_device(): pl.pallas_call(functools.partial(kernel, sizes), out_shape=(jax.ShapeDtyp...  16.9 us
    unnamed x4, local copies, waits for them, and re-layouts  2.11 us

profile of v4, /device:TPU:19, one launch (start us, length us, event | category | flops | bytes accessed | tf_op | source)
XLA Modules:
  0.0 19.6 jit_solution(5200340948537082213)
XLA Ops:
  0.6 0.0 copy-start
  0.6 0.7 %copy-done = f32[8,4,1,128]{3,2,1,0:T(1,128)S(1)} copy-done((f32[8,4,1,128]{3,2,1,0:T(1,128)S(1)}, f32[8,4,1,128]{3,2,1,0:T(1,128)}, u32[]{:S(2)}) %copy-start) | copy-done | bytes 16408
  1.3 16.9 %shard_map.41 = (f32[1024,128]{1,0:T(8,128)S(1)}, f32[32,128]{1,0:T(8,128)S(1)}) custom-call(f32[1024,128]{1,0:T(8,128)} %bitcast.11, f32[32,128]{1,0:T(8,128)S(1)} %bitcast.9), custom_call_target="tpu_custom_call" | custom-call | tf_op jit(solution)/shard_map/pallas_call | solution.py:372
  18.2 0.8 %copy.8 = f32[4,1,128,2,1,128]{5,4,3,2,1,0:T(1,128)} copy(f32[4,1,128,2,1,128]{5,4,3,2,1,0:T(1,128)S(1)} %bitcast.8) | data formatting | bytes 1048576
  19.0 0.6 %copy.9 = f32[8,4,1,128]{3,2,1,0:T(1,128)} copy(f32[8,4,1,128]{3,2,1,0:T(1,128)S(1)} %bitcast.10) | data formatting | bytes 32768
Async XLA Ops:
  0.6 0.7 %copy-start = (f32[8,4,1,128]{3,2,1,0:T(1,128)S(1)}, f32[8,4,1,128]{3,2,1,0:T(1,128)}, u32[]{:S(2)}) copy-start(f32[8,4,1,128]{3,2,1,0:T(1,128)} %param.3) | copy-start | bytes 49156

commit v5 on v4

--- a/solution.py
+++ b/solution.py
@@ -239,7 +239,7 @@
 
     @pl.when(inner)
     def _():
-        for i in range(max(rb, pieces)):
+        for i in range(max(rb, pieces + 2)):
             if i < rb:
                 y_copy(i, 0).wait_recv()
                 for b in range(slots):
@@ -247,10 +247,10 @@
                     def _(i=i, b=b):
                         y_copy(i, b).start()
 
-            if i < pieces:
+            if 2 <= i < pieces + 2:
                 @pl.when(relays)
                 def _(i=i):
-                    relay(i)
+                    relay(i - 2)
 
     def spread(p):
         for head in reversed(range(1, len(heads))):
@@ -315,12 +315,12 @@
         if i == 0:
             flat = jnp.where(r == 0, lead, flat)
         red_ref[pl.ds(i, sides, stride=rb), :] = flat
+    across = dot(w, jnp.concatenate([zbuf[j] for j in range(cb)], axis=1), ((1,), (0,)))
+    change = dot(own, across, ((1,), (0,)))
     for j in range(cb):
-        across = dot(w, zbuf[j], ((1,), (0,)))
-        change = dot(own, across, ((1,), (0,)))
         for i in range(rb):
             here = pl.ds(i * nb * cb + j, nb, stride=cb)
-            block = a_ref[here, :] - change[i * nb : (i + 1) * nb]
+            block = a_ref[here, :] - change[i * nb : (i + 1) * nb, j * nb : (j + 1) * nb]
             if i == 0:
                 block = jnp.where(r == 0, 0.0, block)
             if j == 0:

time: 19.9 us -> 20 us (level)
  no operation moved by 1% of the time
where the time goes in v5:
time: 20 us; the launch traced here: 19.8 us
  Pallas kernels  17 us (85%)
  local copies, waits for them, and re-layouts  2.11 us (11%)
  between operations  0.65 us (3%)
    pallas_call x1, Pallas kernels, on_device(): pl.pallas_call(functools.partial(kernel, sizes), out_shape=(jax.ShapeDtyp...  17 us
    unnamed x4, local copies, waits for them, and re-layouts  2.11 us

profile of v5, /device:TPU:19, one launch (start us, length us, event | category | flops | bytes accessed | tf_op | source)
XLA Modules:
  0.0 19.8 jit_solution(17685018489388336570)
XLA Ops:
  0.6 0.0 copy-start
  0.6 0.7 %copy-done = f32[8,4,1,128]{3,2,1,0:T(1,128)S(1)} copy-done((f32[8,4,1,128]{3,2,1,0:T(1,128)S(1)}, f32[8,4,1,128]{3,2,1,0:T(1,128)}, u32[]{:S(2)}) %copy-start) | copy-done | bytes 16408
  1.3 17.0 %shard_map.41 = (f32[1024,128]{1,0:T(8,128)S(1)}, f32[32,128]{1,0:T(8,128)S(1)}) custom-call(f32[1024,128]{1,0:T(8,128)} %bitcast.11, f32[32,128]{1,0:T(8,128)S(1)} %bitcast.9), custom_call_target="tpu_custom_call" | custom-call | tf_op jit(solution)/shard_map/pallas_call | solution.py:372
  18.4 0.8 %copy.8 = f32[4,1,128,2,1,128]{5,4,3,2,1,0:T(1,128)} copy(f32[4,1,128,2,1,128]{5,4,3,2,1,0:T(1,128)S(1)} %bitcast.8) | data formatting | bytes 1048576
  19.2 0.6 %copy.9 = f32[8,4,1,128]{3,2,1,0:T(1,128)} copy(f32[8,4,1,128]{3,2,1,0:T(1,128)S(1)} %bitcast.10) | data formatting | bytes 32768
Async XLA Ops:
  0.6 0.7 %copy-start = (f32[8,4,1,128]{3,2,1,0:T(1,128)S(1)}, f32[8,4,1,128]{3,2,1,0:T(1,128)}, u32[]{:S(2)}) copy-start(f32[8,4,1,128]{3,2,1,0:T(1,128)} %param.3) | copy-start | bytes 49156

commit v6 on v5

--- a/solution.py
+++ b/solution.py
@@ -226,13 +226,15 @@
                     y_copy(i, b).start()
 
     relays = (r != 0) & (r < row_count - 1)
+    late = relays & (r >= 2) & leads
+    ahead = relays & ~late
     inner = (c != 0) & (child[0] != 0)
 
     def relay(j):
         z_copy(j).wait_recv()
         z_copy(j).start()
 
-    @pl.when(relays & ~inner)
+    @pl.when(ahead & ~inner)
     def _():
         for j in range(pieces):
             relay(j)
@@ -248,7 +250,7 @@
                         y_copy(i, b).start()
 
             if 2 <= i < pieces + 2:
-                @pl.when(relays)
+                @pl.when(ahead)
                 def _(i=i):
                     relay(i - 2)
 
@@ -295,6 +297,11 @@
     def _():
         for p in range(3):
             w_pass(p).wait_recv()
+
+    @pl.when(late)
+    def _():
+        for j in range(pieces):
+            relay(j)
 
     @pl.when((c != 0) & ~inner)
     def _():

time: 20 us -> 19.9 us (level)
  the two profiles are of different devices: /device:TPU:19 before, /device:TPU:26 now
where the time goes in v6:
time: 19.9 us; the launch traced here: 19.6 us
  Pallas kernels  16.9 us (85%)
  local copies, waits for them, and re-layouts  2.11 us (11%)
  between operations  0.65 us (3%)
    pallas_call x1, Pallas kernels, on_device(): pl.pallas_call(functools.partial(kernel, sizes), out_shape=(jax.ShapeDtyp...  16.9 us
    unnamed x4, local copies, waits for them, and re-layouts  2.11 us

profile of v6, /device:TPU:26, one launch (start us, length us, event | category | flops | bytes accessed | tf_op | source)
XLA Modules:
  0.0 19.6 jit_solution(9635342245252413127)
XLA Ops:
  0.6 0.0 copy-start
  0.6 0.7 %copy-done = f32[8,4,1,128]{3,2,1,0:T(1,128)S(1)} copy-done((f32[8,4,1,128]{3,2,1,0:T(1,128)S(1)}, f32[8,4,1,128]{3,2,1,0:T(1,128)}, u32[]{:S(2)}) %copy-start) | copy-done | bytes 16408
  1.3 16.9 %shard_map.41 = (f32[1024,128]{1,0:T(8,128)S(1)}, f32[32,128]{1,0:T(8,128)S(1)}) custom-call(f32[1024,128]{1,0:T(8,128)} %bitcast.11, f32[32,128]{1,0:T(8,128)S(1)} %bitcast.9), custom_call_target="tpu_custom_call" | custom-call | tf_op jit(solution)/shard_map/pallas_call | solution.py:379
  18.2 0.8 %copy.8 = f32[4,1,128,2,1,128]{5,4,3,2,1,0:T(1,128)} copy(f32[4,1,128,2,1,128]{5,4,3,2,1,0:T(1,128)S(1)} %bitcast.8) | data formatting | bytes 1048576
  19.0 0.6 %copy.9 = f32[8,4,1,128]{3,2,1,0:T(1,128)} copy(f32[8,4,1,128]{3,2,1,0:T(1,128)S(1)} %bitcast.10) | data formatting | bytes 32768
Async XLA Ops:
  0.6 0.7 %copy-start = (f32[8,4,1,128]{3,2,1,0:T(1,128)S(1)}, f32[8,4,1,128]{3,2,1,0:T(1,128)}, u32[]{:S(2)}) copy-start(f32[8,4,1,128]{3,2,1,0:T(1,128)} %param.3) | copy-start | bytes 49156
